TPU v7x, 128 devices: a whole 4x4x4 slice. The times are simulated.
128 devices in a mesh: row: 16 (over y_lo, x, core), col: 8 (over z, y_hi).
Axes of the slice: x: 4, y: 4 (y_hi: 2, y_lo: 2; y = y_hi * 2 + y_lo), z: 4, core: 2. Of those that a mesh axis runs over, the one named last changes fastest.
Arguments:
- core_matrix: bfloat16 [8192, 8192], P('row', 'col'), may hold values from -0.1875 to 0.1875
- pattern: int32 [64, 64], P('row', 'col'), may hold values from 0 to 1, as said below
- shift: float32 [1], replicated, may hold values from -1 to 1
- potential: float32 [128, 64, 128], P('row', 'col'), may hold values from -6 to 6
- home: int32 [64], replicated, may hold values from 0 to 127, as said below
- centres: int32 [3, 64, 128], replicated, may hold values from 0 to 127, as said below
- exponents: float32 [64, 128], replicated, may hold values from 0.05 to 1
- extents: int32 [64, 128], replicated, may hold values from 2 to 7
Outputs:
- scaled: bfloat16 [8192, 8192], P('row', 'col')
- square: bfloat16 [8192, 8192], P('row', 'col')
Inputs may be any that keep to these rules, and one draw needn't show every extreme that they name: `pattern`: entries are 0 or 1; every diagonal entry is 1. `home`: at most 2 clusters share a brick, and some brick holds exactly 2. `centres`: the x coordinates lie below 8, the y below 8, the z below 128.
All inputs are finite; a program needn't handle non-finite values.
Results may differ from a plain program's by a relative error of at most 0.0058.
Values may be sent and summed in bfloat16 or wider, within the bound.
No kernel may reach another device: no remote copies, remote signals or barrier semaphores. Data moves between devices by JAX's collectives and lax.ppermute only.
A program may use at most 128 MiB of HBM per device.

v0:
```python
import functools

import jax
import jax.numpy as jnp
from jax import lax
from jax.experimental import pallas as pl
from jax.experimental.pallas import tpu as pltpu
from jax.sharding import PartitionSpec as P

BS = 128
CAP = 20
GROUP = 4
TURN = 4
ORDER = 8192
VOLUME = 0.015625
SUM_LANE = 64
LISTED = 2048 + 32 * GROUP + TURN * GROUP
F32 = jnp.float32
BF16 = jnp.bfloat16


def params(mebibytes):
    return pltpu.CompilerParams(vmem_limit_bytes=mebibytes * 2**20)


def pack_kernel(pattern_ref, place_ref, core_ref, payload_ref, sum_ref):
    first_row = place_ref[0] * 4
    first_col = place_ref[1] * 8
    sum_ref[...] = jnp.zeros_like(sum_ref)

    def put(i, j, slot):
        payload_ref[pl.ds(pl.multiple_of(slot * BS, BS), BS), :] = core_ref[
            i * BS : (i + 1) * BS, j * BS : (j + 1) * BS
        ]

    slot = jnp.int32(0)
    for i in range(4):
        for j in range(8):
            kept = pattern_ref[i, j] != 0

            @pl.when(kept & (slot < CAP))
            def _():
                put(i, j, slot)

            @pl.when(kept & (first_row + i != first_col + j))
            def _():
                block = core_ref[i * BS : (i + 1) * BS, j * BS : (j + 1) * BS].astype(F32)
                squares = (block * block).reshape(16, 8, BS)
                sum_ref[...] += jnp.sum(squares, axis=0)

            slot += kept.astype(jnp.int32)
    for i in range(4):
        for j in range(8):
            dropped = pattern_ref[i, j] == 0

            @pl.when(dropped & (slot < CAP))
            def _():
                put(i, j, slot)

            slot += dropped.astype(jnp.int32)


def brick_kernel(potential_ref, brick_ref):
    brick_ref[...] = potential_ref[...].astype(BF16)


def column(row_values):
    return jnp.broadcast_to(row_values, (BS, BS)).T


def values_kernel(place_ref, centres_ref, exponents_ref, extents_ref, phi_ref, along_ref, slots, sems):
    row, col = place_ref[0], place_ref[1]

    def copy(k):
        return pltpu.make_async_copy(slots.at[k % 2], phi_ref.at[k], sems.at[k % 2])

    def one(k, carry):
        @pl.when(k >= 2)
        def _():
            copy(k - 2).wait()

        cluster = jnp.where(k < 4, row * 4 + k, col * 8 + row % 2 * 4 + k - 4)
        decay = column(exponents_ref[pl.ds(cluster, 1), :])
        reach = column(extents_ref[pl.ds(cluster, 1), :].astype(F32))
        cut = jnp.exp(-decay * (reach * reach + 0.5))
        at_x = column(centres_ref[0, pl.ds(cluster, 1), :].astype(F32))
        at_y = column(centres_ref[1, pl.ds(cluster, 1), :].astype(F32))
        at_z = column(centres_ref[2, pl.ds(cluster, 1), :].astype(F32))
        off_z = lax.broadcasted_iota(jnp.int32, (BS, BS), 1).astype(F32) - at_z
        along_z = jnp.exp(-decay * (off_z * off_z))
        for y in range(8):
            off_y = y - at_y
            along_ref[y] = jnp.exp(-decay * (off_y * off_y))
        for x in range(8):
            off_x = x - at_x
            along_xz = along_z * jnp.exp(-decay * (off_x * off_x))
            for y in range(8):
                phi = along_xz * along_ref[y]
                slots[k % 2, x, :, y * BS : (y + 1) * BS] = jnp.where(phi >= cut, phi, 0.0).astype(BF16)
        copy(k).start()
        return carry

    lax.fori_loop(0, 8, one, 0)
    copy(6).wait()
    copy(7).wait()


def grid_kernel(with_sum, place_ref, home_ref, shift_ref, same_ref, other_ref, phi_ref, *rest):
    if with_sum:
        core_ref, sum_ref, pattern_ref, blocks_ref, total_ref, slots, sems = rest
    else:
        blocks_ref, slots, sems = rest
    row, col = place_ref[0], place_ref[1]
    first = row * 4 if with_sum else col * 8 + row % 2 * 4
    place = 0 if with_sum else 4

    def copy(k):
        return pltpu.make_async_copy(phi_ref.at[place + k], slots.at[k], sems.at[k])

    for k in range(4):
        copy(k).start()

    def one(k, carry):
        home = home_ref[first + k]
        same = (home // 8 ^ row) % 2 == 0
        index = home // 16 * 8 + home % 8
        copy(k).wait()
        total = jnp.zeros((BS, BS), F32)
        for x in range(8):
            slab = slice(x * 8, x * 8 + 8)
            brick = jnp.where(same, same_ref[index, slab, :].astype(F32), other_ref[index, slab, :].astype(F32))
            values = jnp.concatenate([brick[y : y + 1] for y in range(8)], axis=1).astype(BF16)
            phi = slots[k, x]
            total += lax.dot_general(phi * values, phi, (((1,), (1,)), ((), ())), preferred_element_type=F32)
        blocks_ref[k] = (total * VOLUME).astype(BF16)
        return carry

    lax.fori_loop(0, 4, one, 0)
    if with_sum:
        total_ref[...] = jnp.sum(sum_ref[...], axis=0, keepdims=True)

        @pl.when(col == row // 2)
        def _():
            eye = identity()
            for i in range(4):
                corner = pl.multiple_of((row % 2 * 4 + i) * BS, BS)
                block = core_ref[i * BS : (i + 1) * BS, pl.ds(corner, BS)].astype(F32)
                block = block + blocks_ref[i].astype(F32) - shift_ref[0] * eye
                total_ref[...] += jnp.sum(block * block, axis=0, keepdims=True)

        lanes = lax.broadcasted_iota(jnp.int32, (1, BS), 1)
        note = jnp.where(lanes == SUM_LANE, jnp.sum(total_ref[...], axis=1, keepdims=True), 0.0)
        for i in range(4):
            for j in range(8):
                note = jnp.where(lanes == i * 8 + j, pattern_ref[i, j].astype(F32), note)
        total_ref[...] = note


def identity():
    rows = lax.broadcasted_iota(jnp.int32, (BS, BS), 0)
    columns = lax.broadcasted_iota(jnp.int32, (BS, BS), 1)
    return (rows == columns).astype(F32)


def plan_kernel(
    place_ref, notes_ref, turns_ref, out_ref, left_ref, right_ref, most_ref, slots_ref, slots, kept_left, kept_right, kept_at, sem
):
    row, col = place_ref[0], place_ref[1]
    lanes = lax.broadcasted_iota(jnp.int32, (BS, BS), 1)
    kept = jnp.where(lanes < 32, notes_ref[...], 0.0).T
    earlier = lax.broadcasted_iota(jnp.int32, (BS, BS), 1) < lax.broadcasted_iota(jnp.int32, (BS, BS), 0)
    before = jnp.dot(earlier.astype(BF16), kept.astype(BF16), preferred_element_type=F32)
    slots_ref[...] = jnp.where(kept > 0.5, before, -1.0)[:40].astype(jnp.int32)
    most_ref[0] = jnp.max(jnp.sum(kept, axis=0, keepdims=True)).astype(jnp.int32)
    copy = pltpu.make_async_copy(slots_ref, slots, sem)
    copy.start()
    copy.wait()

    def block_row(i, number):
        def piece(other, count):
            device = row * 8 + other
            base = ((other ^ col) % 2 * 4 + (other // 2 - col // 2) % 4) * CAP
            right = ((other // 4 ^ row // 8) * 4 + (other - row // 2) % 4) * 2 * CAP
            for j in range(8):
                slot = slots[i * 8 + j, device]
                kept_left[count] = base + slot
                kept_right[count] = right + j // 4 * CAP
                kept_at[count] = j % 4 * 8 * BS + (other * 2 + j // 4) * 8 + col
                count += (slot >= 0).astype(jnp.int32)
            return count

        count = lax.fori_loop(0, 8, piece, jnp.int32(0))
        for more in range(3):
            kept_left[count + more] = 0
            kept_right[count + more] = 0
            kept_at[count + more] = 32 * BS

        def block(j, number):
            def listing(number):
                start = number // GROUP
                def four(n, number):
                    for inner in range(4):
                        at = kept_at[n * 4 + inner] + j * BS
                        slot = slots[at >> 7, at & 127]
                        left_ref[number] = kept_left[n * 4 + inner]
                        right_ref[number] = kept_right[n * 4 + inner] + slot
                        number += (slot >= 0).astype(jnp.int32)
                    return number

                number = lax.fori_loop(0, (count + 3) // 4, four, number)
                for more in range(GROUP - 1):
                    left_ref[number + more] = 8 * CAP
                    right_ref[number + more] = 0
                end = (number + GROUP - 1) // GROUP

                def name(group, carry):
                    out_ref[group] = i * 8 + j
                    return carry

                lax.fori_loop(start, end, name, 0)
                return end * GROUP

            wanted = slots[i * 8 + j, row * 8 + col] >= 0
            return lax.cond(wanted, listing, lambda n: n, number)

        return lax.fori_loop(0, 8, block, number)

    number = lax.fori_loop(0, 4, block_row, jnp.int32(0))
    groups = number // GROUP
    for more in range(TURN):
        out_ref[groups + more] = 32
        for inner in range(GROUP):
            left_ref[number + more * GROUP + inner] = 8 * CAP
            right_ref[number + more * GROUP + inner] = 0
    turns_ref[0] = (groups + TURN - 1) // TURN


def scaling(frob_ref):
    lanes = lax.broadcasted_iota(jnp.int32, (BS, BS), 1)
    total = jnp.sum(jnp.where(lanes == SUM_LANE, frob_ref[...], 0.0), axis=(0, 1), keepdims=True)
    return lax.rsqrt(total / ORDER + 1e-6)


def prepare_kernel(
    place_ref, pattern_ref, shift_ref, frob_ref, core_ref, row_grid_ref, col_own_ref, col_other_ref, scaled_ref,
    linear_ref, col_grid_ref
):
    first_row = place_ref[0] * 4
    first_col = place_ref[1] * 8
    core = place_ref[0] % 2
    for n in range(4):
        col_grid_ref[core * 4 + n] = col_own_ref[n]
        col_grid_ref[(1 - core) * 4 + n] = col_other_ref[n]
    shift = shift_ref[0]
    scale = scaling(frob_ref)
    eye = identity()
    dot = functools.partial(jnp.dot, preferred_element_type=F32)
    for i in range(4):
        for j in range(8):
            block = (slice(i * BS, (i + 1) * BS), slice(j * BS, (j + 1) * BS))
            kept = pattern_ref[i, j] != 0
            diagonal = first_row + i == first_col + j

            @pl.when(kept)
            def _():
                here = core_ref[block]
                wide = here.astype(F32)
                linear_ref[i * 8 + j] = dot(row_grid_ref[i], here) + dot(here, col_grid_ref[j]) - 2.0 * shift * wide

                @pl.when(diagonal)
                def _():
                    grid = row_grid_ref[i]
                    grid_wide = grid.astype(F32)
                    linear_ref[i * 8 + j] += dot(grid, grid) - 2.0 * shift * grid_wide + shift * shift * eye
                    scaled_ref[block] = ((wide + grid_wide - shift * eye) * scale).astype(BF16)

                @pl.when(jnp.logical_not(diagonal))
                def _():
                    scaled_ref[block] = (wide * scale).astype(BF16)

            @pl.when(jnp.logical_not(kept))
            def _():
                scaled_ref[block] = jnp.zeros((BS, BS), BF16)


def product_kernel(
    place_ref, pattern_ref, turns_ref, out_ref, left_ref, right_ref, frob_ref, linear_ref, *rest
):
    payload, crossed, own_role, other_role, halves = rest[0], rest[1], rest[2:9], rest[9:16], rest[16:18]
    square_ref, left_all, right_all, acc_ref, sems = rest[18:]
    core = place_ref[0] % 2

    def part(whole, at, size, source, number):
        return pltpu.make_async_copy(source, whole.at[pl.ds(at, size)], sems.at[number])

    copies = [
        part(left_all, 0, CAP, payload, 0),
        part(right_all, core * CAP, CAP, payload, 1),
        part(right_all, (1 - core) * CAP, CAP, crossed, 2),
    ]
    for copy in copies:
        copy.start()
    along_x = {1: 0, 2: 2, 3: 1, 4: 3, 5: 5, 6: 6, 7: 4}
    along_z = {1: 0, 2: 2, 3: 1, 4: 4, 5: 5, 7: 6}
    low, high = halves
    for k in range(1, 8):
        of_core_0 = [part(right_all, 2 * k * CAP, 2 * CAP, own_role[along_x[k]], 2 + 2 * k)]
        of_core_1 = [part(right_all, 2 * k * CAP, 2 * CAP, other_role[along_x[k]], 2 + 2 * k)]
        if k == 6:
            of_core_0.append(part(left_all, k * CAP, CAP, high, 1 + 2 * k))
            of_core_1.append(part(left_all, k * CAP, CAP, low, 1 + 2 * k))
        else:
            theirs, mine = other_role[along_z[k]], own_role[along_z[k]]
            of_core_0.append(part(left_all, k * CAP, CAP, theirs.at[pl.ds(CAP, CAP)], 1 + 2 * k))
            of_core_1.append(part(left_all, k * CAP, CAP, mine.at[pl.ds(0, CAP)], 1 + 2 * k))
        copies += of_core_0

        @pl.when(core == 0)
        def _():
            for copy in of_core_0:
                copy.start()

        @pl.when(core == 1)
        def _():
            for copy in of_core_1:
                copy.start()

    left_all[8 * CAP] = jnp.zeros((BS, BS), BF16)
    acc_ref[...] = jnp.zeros_like(acc_ref)
    scale = scaling(frob_ref)
    dot = functools.partial(jnp.dot, preferred_element_type=F32)
    for i in range(4):
        for j in range(8):

            @pl.when(pattern_ref[i, j] == 0)
            def _():
                square_ref[i * BS : (i + 1) * BS, j * BS : (j + 1) * BS] = jnp.zeros((BS, BS), BF16)

    for copy in copies:
        copy.wait()

    def turn(t, carry):
        sums = []
        for group in range(TURN):
            at = [(t * TURN + group) * GROUP + n for n in range(GROUP)]
            left = jnp.concatenate([left_all[left_ref[n]] for n in at], axis=1)
            right = jnp.concatenate([right_all[right_ref[n]] for n in at], axis=0)
            sums.append(dot(left, right))
        for group in range(TURN):
            acc_ref[out_ref[t * TURN + group]] += sums[group]
        return carry

    lax.fori_loop(0, turns_ref[0], turn, 0)
    for i in range(4):
        for j in range(8):
            block = (slice(i * BS, (i + 1) * BS), slice(j * BS, (j + 1) * BS))

            @pl.when(pattern_ref[i, j] != 0)
            def _():
                square_ref[block] = ((acc_ref[i * 8 + j] + linear_ref[i * 8 + j]) * (scale * scale)).astype(BF16)


VM = pl.BlockSpec(memory_space=pltpu.VMEM)
SM = pl.BlockSpec(memory_space=pltpu.SMEM)
ANY = pl.BlockSpec(memory_space=pl.ANY)
HBM = pl.BlockSpec(memory_space=pltpu.HBM)


def to_all(value, axis, count, groups=None):
    copies = jnp.broadcast_to(value[None], (count,) + value.shape)
    return lax.all_to_all(copies, axis, 0, 0, axis_index_groups=groups)


def place_of(device):
    row, col = device // 8, device % 8
    return row // 2 % 4, col % 2 * 2 + row // 8, col // 2, row % 2


def device_of(x, y, z, core):
    return ((y % 2 * 4 + x % 4) * 2 + core) * 8 + z % 4 * 2 + y // 2


def move(value, where):
    return lax.ppermute(value, ("row", "col"), [(k, device_of(*where(*place_of(k)))) for k in range(128)])


def ring(value, off):
    return move(value, lambda x, y, z, core: (x, y, z - off, core) if core else (x - off, y, z, core))


def across_y(value):
    return move(value, lambda x, y, z, core: (x, 3 - y if core else y ^ 1, z, core))


def across_y_again(value):
    return move(value, lambda x, y, z, core: (x, y ^ 1, z, core) if core else (x + 1, y, z, core))


def from_core_1(value, off, core):
    pairs = []
    for k in range(128):
        x, y, z, source = place_of(k)
        if source == 1:
            pairs.append((k, device_of(x, y, z - off, core)))
    return lax.ppermute(value, ("row", "col"), pairs)


def to_core(value):
    return lax.ppermute(value, "row", [(k, k ^ 1) for k in range(16)])


def lasting(microseconds):
    return pl.CostEstimate(flops=int(microseconds * 1e9), bytes_accessed=2**20, transcendentals=0)


def body(core_matrix, pattern, shift, potential, home, centres, exponents, extents):
    row = lax.axis_index("row")
    col = lax.axis_index("col")
    place = jnp.stack([row, col]).astype(jnp.int32)

    brick = pl.pallas_call(
        brick_kernel,
        in_specs=[VM],
        out_specs=VM,
        out_shape=jax.ShapeDtypeStruct((64, BS), BF16),
        compiler_params=params(4),
        cost_estimate=lasting(1),
        name="brick",
    )(potential.reshape(64, BS))
    same_core = [[row * 8 + col for row in range(core, 16, 2) for col in range(8)] for core in range(2)]
    half = to_all(brick, ("row", "col"), 64, same_core)

    (core_after_brick, _) = lax.optimization_barrier((core_matrix, brick))
    payload, squares = pl.pallas_call(
        pack_kernel,
        in_specs=[SM, SM, VM],
        out_specs=[VM, VM],
        out_shape=[jax.ShapeDtypeStruct((CAP * BS, BS), BF16), jax.ShapeDtypeStruct((8, BS), F32)],
        compiler_params=params(4),
        cost_estimate=lasting(2),
        name="pack",
    )(pattern, place, core_after_brick)
    payload = payload.reshape(CAP, BS, BS)
    crossed = to_core(payload)

    pair = jnp.concatenate([payload, crossed])
    step = across_y(pair)
    after, before = ring(pair, 1), ring(pair, -1)
    phi = pl.pallas_call(
        values_kernel,
        in_specs=[SM, VM, VM, VM],
        out_specs=HBM,
        out_shape=jax.ShapeDtypeStruct((8, 8, BS, 8 * BS), BF16),
        scratch_shapes=[
            pltpu.VMEM((8, BS, BS), F32),
            pltpu.VMEM((2, 8, BS, 8 * BS), BF16),
            pltpu.SemaphoreType.DMA((2,)),
        ],
        compiler_params=params(49),
        cost_estimate=lasting(10),
        name="values",
    )(place, centres, exponents, extents)

    half, phi, step, after, before = lax.optimization_barrier((half, phi, step, after, before))

    far = ring(after, 1)
    second = across_y_again(step)
    bricks = [half, to_core(half)]

    def grid_blocks(with_sum, *more):
        extra = [VM, VM, SM] if with_sum else []
        out_shape = [jax.ShapeDtypeStruct((4, BS, BS), BF16)]
        if with_sum:
            out_shape.append(jax.ShapeDtypeStruct((1, BS), F32))
        return pl.pallas_call(
            functools.partial(grid_kernel, with_sum),
            in_specs=[SM, SM, SM, VM, VM, HBM] + extra,
            out_specs=[VM] * len(out_shape),
            out_shape=out_shape,
            scratch_shapes=[pltpu.VMEM((4, 8, BS, 8 * BS), BF16), pltpu.SemaphoreType.DMA((4,))],
            compiler_params=params(49),
            cost_estimate=lasting(5),
            name="grid_rows" if with_sum else "grid_cols",
        )(place, home, shift, *bricks, phi, *more)

    row_grid, total = grid_blocks(True, core_matrix, squares, pattern)
    crossings = [to_core(after), to_core(before)]
    frob = to_all(total, ("row", "col"), 128).reshape(128, BS)
    partner = jnp.where(row % 2 == 0, step, second)
    after, before, far, step, second, partner, row_grid, frob, *rest = lax.optimization_barrier(
        (after, before, far, step, second, partner, row_grid, frob, *bricks, *crossings)
    )
    bricks, crossings = rest[:2], rest[2:]

    third = ring(second, -1)
    other_after = ring(partner, 1)
    crossings += [to_core(far), to_core(step), to_core(second)]
    (col_grid,) = grid_blocks(False)
    *listed, most = pl.pallas_call(
        plan_kernel,
        in_specs=[SM, VM],
        out_specs=[SM] * 5,
        out_shape=[
            jax.ShapeDtypeStruct((1,), jnp.int32),
            jax.ShapeDtypeStruct((LISTED // GROUP,), jnp.int32),
            jax.ShapeDtypeStruct((LISTED,), jnp.int32),
            jax.ShapeDtypeStruct((LISTED,), jnp.int32),
            jax.ShapeDtypeStruct((1,), jnp.int32),
        ],
        scratch_shapes=[pltpu.VMEM((40, BS), jnp.int32), pltpu.SMEM((40, BS), jnp.int32)]
        + [pltpu.SMEM((72,), jnp.int32)] * 3
        + [pltpu.SemaphoreType.DMA],
        compiler_params=params(4),
        cost_estimate=lasting(9),
        name="plan",
    )(place, frob)
    other_after, third, col_grid, *rest = lax.optimization_barrier(
        (other_after, third, col_grid, *crossings, *listed)
    )
    crossings, listed = rest[:5], rest[5:]

    low, high = from_core_1(third[:CAP], -1, 1), from_core_1(other_after[CAP:], 1, 0)
    crossings += [to_core(other_after), to_core(third)]
    col_grid_crossed = to_core(col_grid)
    scaled, linear = pl.pallas_call(
        prepare_kernel,
        in_specs=[SM] * 3 + [VM] * 5,
        out_specs=[VM, VM],
        out_shape=[jax.ShapeDtypeStruct((512, 1024), BF16), jax.ShapeDtypeStruct((32, BS, BS), F32)],
        scratch_shapes=[pltpu.VMEM((8, BS, BS), BF16)],
        compiler_params=params(4),
        cost_estimate=lasting(4),
        name="prepare",
    )(place, pattern, shift, frob, core_matrix, row_grid, col_grid, col_grid_crossed)
    low, high, scaled, linear, *crossings = lax.optimization_barrier((low, high, scaled, linear, *crossings))

    halves = [low, high]
    own_role = [after, before, far, step, second, other_after, third]
    overflow = most[0] > CAP

    def sparse():
        return pl.pallas_call(
            product_kernel,
            in_specs=[SM] * 6 + [VM] * 2 + [ANY] * 18,
            out_specs=VM,
            out_shape=jax.ShapeDtypeStruct((512, 1024), BF16),
            scratch_shapes=[
                pltpu.VMEM((8 * CAP + 1, BS, BS), BF16),
                pltpu.VMEM((16 * CAP, BS, BS), BF16),
                pltpu.VMEM((33, BS, BS), F32),
                pltpu.SemaphoreType.DMA((18,)),
            ],
            compiler_params=params(24),
            cost_estimate=lasting(12),
            name="product",
        )(place, pattern, *listed, frob, linear, payload, crossed, *own_role, *crossings, *halves)

    def dense():
        keep = pattern.astype(F32)[:, None, :, None]
        product = jnp.dot(
            lax.all_gather(scaled, "col", axis=1, tiled=True),
            lax.all_gather(scaled, "row", axis=0, tiled=True),
            preferred_element_type=F32,
        )
        return (product.reshape(4, BS, 8, BS) * keep).reshape(512, 1024).astype(BF16)

    return scaled, lax.cond(overflow, dense, sparse)


def solution(mesh):
    in_specs = (P("row", "col"), P("row", "col"), P(), P("row", "col", None), P(), P(), P(), P())
    out_specs = (P("row", "col"), P("row", "col"))
    return jax.shard_map(body, mesh=mesh, in_specs=in_specs, out_specs=out_specs, check_vma=False)
```

profile of v0, /device:TPU:1, one launch (start us, length us, event | category | flops | bytes accessed | tf_op | source)
XLA Modules:
  0.0 128.9 jit_solution(13076429721335159068)
XLA Ops:
  10.7 1.5 %collective-permute-start = (bf16[20,128,128]{2,1,0:T(8,128)(2,1)S(1)}, bf16[20,128,128]{2,1,0:T(8,128)(2,1)S(1)}, u32[]{:S(2)}, u32[]{:S(2)}) collective-permute-start(bf16[20,128,128]{2,1,0:T(8,128)(2,1)S(1)} %bitcast.18), channel_id=1, source_target_pairs={{0,8},{8,0},{16,24},{24,16},{32,40},{40,32},{48,56},{56,48},{64,72... | collective-permute-start | bytes 1966088 | tf_op jit(solution)/shard_map/ppermute | solution.py:409
  12.2 1.7 %collective-permute-done = bf16[20,128,128]{2,1,0:T(8,128)(2,1)S(1)} collective-permute-done((bf16[20,128,128]{2,1,0:T(8,128)(2,1)S(1)}, bf16[20,128,128]{2,1,0:T(8,128)(2,1)S(1)}, u32[]{:S(2)}, u32[]{:S(2)}) %collective-permute-start) | collective-permute-done | bytes 655392 | tf_op jit(solution)/shard_map/ppermute | solution.py:409
  15.2 1.8 %collective-permute-start.3 = (bf16[40,128,128]{2,1,0:T(8,128)(2,1)}, bf16[40,128,128]{2,1,0:T(8,128)(2,1)}, u32[]{:S(2)}, u32[]{:S(2)}) collective-permute-start(bf16[40,128,128]{2,1,0:T(8,128)(2,1)} %pad_maximum_fusion), channel_id=1, source_target_pairs={{0,16},{1,17},{2,18},{3,19},{4,20},{5,21},{6,22},{7,23},{8,10},{9,... | collective-permute-start | bytes 3932168 | tf_op jit(solution)/shard_map/ppermute | solution.py:384
  17.0 2.1 %collective-permute-start.2 = (bf16[40,128,128]{2,1,0:T(8,128)(2,1)}, bf16[40,128,128]{2,1,0:T(8,128)(2,1)}, u32[]{:S(2)}, u32[]{:S(2)}) collective-permute-start(bf16[40,128,128]{2,1,0:T(8,128)(2,1)} %pad_maximum_fusion), channel_id=1, source_target_pairs={{0,48},{1,49},{2,50},{3,51},{4,52},{5,53},{6,54},{7,55},{8,14},{9,... | collective-permute-start | bytes 3932168 | tf_op jit(solution)/shard_map/ppermute | solution.py:384
  19.1 2.7 %collective-permute-start.1 = (bf16[40,128,128]{2,1,0:T(8,128)(2,1)}, bf16[40,128,128]{2,1,0:T(8,128)(2,1)}, u32[]{:S(2)}, u32[]{:S(2)}) collective-permute-start(bf16[40,128,128]{2,1,0:T(8,128)(2,1)} %pad_maximum_fusion), channel_id=1, source_target_pairs={{0,64},{1,65},{2,66},{3,67},{4,68},{5,69},{6,70},{7,71},{8,73},{9,... | collective-permute-start | bytes 3932168 | tf_op jit(solution)/shard_map/ppermute | solution.py:384
  23.0 6.5 %all-to-all-start = ((bf16[64,64,128]{2,1,0:T(8,128)(2,1)}), bf16[64,64,128]{2,1,0:T(8,128)(2,1)S(1)}, u32[]{:S(2)}, u32[]{:S(2)}) async-start(bf16[64,64,128]{2,1,0:T(8,128)(2,1)} %broadcast_in_dim.6), calls=%async_computation | async-start | bytes 2097152 | tf_op jit(solution)/shard_map/all_to_all | solution.py:371
  29.5 10.3 %values.1.phi_ref = bf16[8,8,128,1024]{3,2,1,0:T(8,128)(2,1)} custom-call(s32[2]{0:T(128)S(1)} %pad_add_fusion.place_ref, s32[3,64,128]{2,1,0:T(8,128)S(1)} %copy-done.2, f32[64,128]{1,0:T(8,128)S(1)} %copy-done.4, s32[64,128]{1,0:T(8,128)S(1)} %copy-done.5), custom_call_target="tpu_custom_call" | custom-call | flops 10000000000 | bytes 1048576 | tf_op jit(solution)/shard_map/values/pallas_call | solution.py:449
  39.8 8.7 %all-to-all-done.same_ref = bf16[64,64,128]{2,1,0:T(8,128)(2,1)S(1)} async-done(((bf16[64,64,128]{2,1,0:T(8,128)(2,1)}), bf16[64,64,128]{2,1,0:T(8,128)(2,1)S(1)}, u32[]{:S(2)}, u32[]{:S(2)}) %all-to-all-start) | async-done | bytes 1048608 | tf_op jit(solution)/shard_map/all_to_all | solution.py:371
  48.5 5.3 %collective-permute-start.6 = (bf16[64,64,128]{2,1,0:T(8,128)(2,1)S(1)}, bf16[64,64,128]{2,1,0:T(8,128)(2,1)S(1)}, u32[]{:S(2)}, u32[]{:S(2)}) collective-permute-start(bf16[64,64,128]{2,1,0:T(8,128)(2,1)S(1)} %all-to-all-done.same_ref), channel_id=1, source_target_pairs={{0,8},{8,0},{16,24},{24,16},{32,40},{40,32},{48,56},{56,48},{64,72... | collective-permute-start | bytes 3145736 | tf_op jit(solution)/shard_map/ppermute | solution.py:409
  56.1 5.3 %grid_rows.1 = (bf16[4,128,128]{2,1,0:T(8,128)(2,1)S(1)}, f32[1,128]{1,0:T(1,128)S(1)}) custom-call(s32[2]{0:T(128)S(1)} %pad_add_fusion.place_ref, s32[64]{0:T(128)S(1)} %copy-done.1, f32[1]{0:T(128)S(6)} %copy.14.shift_ref, bf16[64,64,128]{2,1,0:T(8,128)(2,1)S(1)} %all-to-all-done.same_ref, bf16[64,64,128]{2,1,0:T(8,128)(2,1)S(1)} %collective-permute-done.6.other_ref, ...), custom_call_target="tpu_custom_call" | custom-call | flops 5000000000 | bytes 1048576 | tf_op jit(solution)/shard_map/grid_rows/pallas_call | solution.py:475
  62.0 5.6 %all-to-all-start.1 = ((f32[128,1,128]{2,1,0:T(1,128)}), f32[128,1,128]{2,1,0:T(1,128)S(1)}, u32[]{:S(2)}, u32[]{:S(2)}) async-start(f32[128,1,128]{2,1,0:T(1,128)} %broadcast_in_dim.8), calls=%async_computation.1 | async-start | bytes 131072 | tf_op jit(solution)/shard_map/all_to_all | solution.py:371
  67.6 3.3 %collective-permute-done.5 = bf16[40,128,128]{2,1,0:T(8,128)(2,1)} collective-permute-done((bf16[40,128,128]{2,1,0:T(8,128)(2,1)}, bf16[40,128,128]{2,1,0:T(8,128)(2,1)}, u32[]{:S(2)}, u32[]{:S(2)}) %collective-permute-start.5) | collective-permute-done | bytes 1310752 | tf_op jit(solution)/shard_map/ppermute | solution.py:384
  71.0 2.6 %broadcast_select_fusion = bf16[40,128,128]{2,1,0:T(8,128)(2,1)} fusion(bf16[40,128,128]{2,1,0:T(8,128)(2,1)} %collective-permute-done.1, bf16[40,128,128]{2,1,0:T(8,128)(2,1)} %collective-permute-done.5, pred[]{:T(512)S(6)} %eq.5), kind=kLoop, calls=%fused_computation.3 | loop fusion | flops 655360 | bytes 3932161 | tf_op jit(solution)/shard_map/jit(_where)/select_n | solution.py:489
  73.6 3.5 %all-to-all-done.1 = f32[128,1,128]{2,1,0:T(1,128)S(1)} async-done(((f32[128,1,128]{2,1,0:T(1,128)}), f32[128,1,128]{2,1,0:T(1,128)S(1)}, u32[]{:S(2)}, u32[]{:S(2)}) %all-to-all-start.1) | async-done | bytes 65568 | tf_op jit(solution)/shard_map/all_to_all | solution.py:371
  78.8 2.1 %collective-permute-start.9 = (bf16[40,128,128]{2,1,0:T(8,128)(2,1)}, bf16[40,128,128]{2,1,0:T(8,128)(2,1)S(1)}, u32[]{:S(2)}, u32[]{:S(2)}) collective-permute-start(bf16[40,128,128]{2,1,0:T(8,128)(2,1)} %broadcast_select_fusion), channel_id=1, source_target_pairs={{0,48},{1,49},{2,50},{3,51},{4,52},{5,53},{6,54},{7,55},{8,14},{9,... | collective-permute-start | bytes 3932168 | tf_op jit(solution)/shard_map/ppermute | solution.py:384
  81.6 5.0 %grid_cols.1.col_own_ref = bf16[4,128,128]{2,1,0:T(8,128)(2,1)S(1)} custom-call(s32[2]{0:T(128)S(1)} %pad_add_fusion.place_ref, s32[64]{0:T(128)S(1)} %copy-done.1, f32[1]{0:T(128)S(6)} %copy.14.shift_ref, bf16[64,64,128]{2,1,0:T(8,128)(2,1)S(1)} %all-to-all-done.same_ref, bf16[64,64,128]{2,1,0:T(8,128)(2,1)S(1)} %collective-permute-done.6.other_ref, ...), custom_call_target="tpu_custom_call" | custom-call | flops 5000000000 | bytes 1048576 | tf_op jit(solution)/shard_map/grid_cols/pallas_call | solution.py:475
  86.6 7.6 %plan.1 = (s32[1]{0:T(128)}, s32[548]{0:T(1024)S(1)}, s32[2192]{0:T(1024)S(1)}, s32[2192]{0:T(1024)S(1)}, s32[1]{0:T(128)}) custom-call(s32[2]{0:T(128)S(1)} %pad_add_fusion.place_ref, f32[128,128]{1,0:T(8,128)S(1)} %bitcast.21), custom_call_target="tpu_custom_call" | custom-call | flops 8999999488 | bytes 1048576 | tf_op jit(solution)/shard_map/plan/pallas_call | solution.py:499
  94.2 1.6 %collective-permute-done.9 = bf16[40,128,128]{2,1,0:T(8,128)(2,1)S(1)} collective-permute-done((bf16[40,128,128]{2,1,0:T(8,128)(2,1)}, bf16[40,128,128]{2,1,0:T(8,128)(2,1)S(1)}, u32[]{:S(2)}, u32[]{:S(2)}) %collective-permute-start.9) | collective-permute-done | bytes 1310752 | tf_op jit(solution)/shard_map/ppermute | solution.py:384
  97.5 4.0 %collective-permute-start.15 = (bf16[20,128,128]{2,1,0:T(8,128)(2,1)S(1)}, bf16[20,128,128]{2,1,0:T(8,128)(2,1)S(1)}, u32[]{:S(2)}, u32[]{:S(2)}) collective-permute-start(bf16[20,128,128]{2,1,0:T(8,128)(2,1)S(1)} %slice.7), channel_id=1, source_target_pairs={{8,6},{9,7},{10,0},{11,1},{12,2},{13,3},{14,4},{15,5},{24,22},{25,... | collective-permute-start | bytes 1966088 | tf_op jit(solution)/shard_map/ppermute | solution.py:405
  101.5 1.9 %collective-permute-start.14 = (bf16[20,128,128]{2,1,0:T(8,128)(2,1)S(1)}, bf16[20,128,128]{2,1,0:T(8,128)(2,1)S(1)}, u32[]{:S(2)}, u32[]{:S(2)}) collective-permute-start(bf16[20,128,128]{2,1,0:T(8,128)(2,1)S(1)} %slice.6), channel_id=1, source_target_pairs={{8,10},{9,11},{10,12},{11,13},{12,14},{13,15},{14,8},{15,9},{24,26... | collective-permute-start | bytes 1966088 | tf_op jit(solution)/shard_map/ppermute | solution.py:405
  105.0 4.2 %prepare.1 = (bf16[512,1024]{1,0:T(8,128)(2,1)}, f32[32,128,128]{2,1,0:T(8,128)S(1)}) custom-call(s32[2]{0:T(128)S(1)} %pad_add_fusion.place_ref, s32[4,8]{1,0:T(4,128)S(1)} %copy-done.10, f32[1]{0:T(128)S(6)} %copy.14.shift_ref, f32[128,128]{1,0:T(8,128)S(1)} %bitcast.22, bf16[512,1024]{1,0:T(8,128)(2,1)S(1)} %copy-done, ...), custom_call_target="tpu_custom_call" | custom-call | flops 4000000000 | bytes 1048576 | tf_op jit(solution)/shard_map/prepare/pallas_call | solution.py:525
  109.2 4.8 %collective-permute-done.14 = bf16[20,128,128]{2,1,0:T(8,128)(2,1)S(1)} collective-permute-done((bf16[20,128,128]{2,1,0:T(8,128)(2,1)S(1)}, bf16[20,128,128]{2,1,0:T(8,128)(2,1)S(1)}, u32[]{:S(2)}, u32[]{:S(2)}) %collective-permute-start.14) | collective-permute-done | bytes 655392 | tf_op jit(solution)/shard_map/ppermute | solution.py:405
  114.0 7.1 %conditional.1 = (bf16[512,1024]{1,0:T(8,128)(2,1)S(1)}) conditional(s32[]{:T(128)} %bitcast.6, (s32[2]{0:T(128)S(1)}, s32[4,8]{1,0:T(4,128)S(1)}, s32[1]{0:T(128)}, s32[548]{0:T(1024)S(1)}, s32[2192]{0:T(1024)S(1)}, /*index=5*/s32[2192]{0:T(1024)S(1)}, f32[128,128]{1,0:T(8,128)S(1)}, f32[32,128,128]{2,1,0:T(8,128)S(1)}, ...), branch_computations={%region_0.1_spmd, %region_1.2_spmd} | conditional | flops 12000000000 | bytes 112198104 | solution.py:567
  114.1 7.1 %product.1 = bf16[512,1024]{1,0:T(8,128)(2,1)S(1)} custom-call(s32[2]{0:T(128)S(1)} %get-tuple-element.56.place_ref, s32[4,8]{1,0:T(4,128)S(1)} %get-tuple-element.60.pattern_ref, s32[1]{0:T(128)} %get-tuple-element.61.turns_ref, s32[548]{0:T(1024)S(1)} %get-tuple-element.62.out_ref, s32[2192]{0:T(1024)S(1)} %get-tuple-element.63.left_ref, ...), custom_call_target="tpu_custom_call" | custom-call | flops 12000000000 | bytes 1048576 | tf_op jit(solution)/shard_map/cond/branch_0_fun/product/pallas_call | solution.py:542
  (58 shorter events, 14.3 us)
Async XLA Ops:
  10.7 3.2 %collective-permute-start = (bf16[20,128,128]{2,1,0:T(8,128)(2,1)S(1)}, bf16[20,128,128]{2,1,0:T(8,128)(2,1)S(1)}, u32[]{:S(2)}, u32[]{:S(2)}) collective-permute-start(bf16[20,128,128]{2,1,0:T(8,128)(2,1)S(1)} %bitcast.18), channel_id=1, source_target_pairs={{0,8},{8,0},{16,24},{24,16},{32,40},{40,32},{48,56},{56,48},{64,72... | collective-permute-start | bytes 1966088 | tf_op jit(solution)/shard_map/ppermute | solution.py:409
  15.2 33.3 %collective-permute-start.3 = (bf16[40,128,128]{2,1,0:T(8,128)(2,1)}, bf16[40,128,128]{2,1,0:T(8,128)(2,1)}, u32[]{:S(2)}, u32[]{:S(2)}) collective-permute-start(bf16[40,128,128]{2,1,0:T(8,128)(2,1)} %pad_maximum_fusion), channel_id=1, source_target_pairs={{0,16},{1,17},{2,18},{3,19},{4,20},{5,21},{6,22},{7,23},{8,10},{9,... | collective-permute-start | bytes 3932168 | tf_op jit(solution)/shard_map/ppermute | solution.py:384
  17.0 31.5 %collective-permute-start.2 = (bf16[40,128,128]{2,1,0:T(8,128)(2,1)}, bf16[40,128,128]{2,1,0:T(8,128)(2,1)}, u32[]{:S(2)}, u32[]{:S(2)}) collective-permute-start(bf16[40,128,128]{2,1,0:T(8,128)(2,1)} %pad_maximum_fusion), channel_id=1, source_target_pairs={{0,48},{1,49},{2,50},{3,51},{4,52},{5,53},{6,54},{7,55},{8,14},{9,... | collective-permute-start | bytes 3932168 | tf_op jit(solution)/shard_map/ppermute | solution.py:384
  19.1 29.4 %collective-permute-start.1 = (bf16[40,128,128]{2,1,0:T(8,128)(2,1)}, bf16[40,128,128]{2,1,0:T(8,128)(2,1)}, u32[]{:S(2)}, u32[]{:S(2)}) collective-permute-start(bf16[40,128,128]{2,1,0:T(8,128)(2,1)} %pad_maximum_fusion), channel_id=1, source_target_pairs={{0,64},{1,65},{2,66},{3,67},{4,68},{5,69},{6,70},{7,71},{8,73},{9,... | collective-permute-start | bytes 3932168 | tf_op jit(solution)/shard_map/ppermute | solution.py:384
  23.0 25.4 %all-to-all-start = ((bf16[64,64,128]{2,1,0:T(8,128)(2,1)}), bf16[64,64,128]{2,1,0:T(8,128)(2,1)S(1)}, u32[]{:S(2)}, u32[]{:S(2)}) async-start(bf16[64,64,128]{2,1,0:T(8,128)(2,1)} %broadcast_in_dim.6), calls=%async_computation | async-start | bytes 2097152 | tf_op jit(solution)/shard_map/all_to_all | solution.py:371
  29.5 26.6 %copy-start.1 = (s32[64]{0:T(128)S(1)}, s32[64]{0:T(128)}, u32[]{:S(2)}) copy-start(s32[64]{0:T(128)} %home_ref.3) | copy-start | bytes 772
  48.5 7.6 %collective-permute-start.6 = (bf16[64,64,128]{2,1,0:T(8,128)(2,1)S(1)}, bf16[64,64,128]{2,1,0:T(8,128)(2,1)S(1)}, u32[]{:S(2)}, u32[]{:S(2)}) collective-permute-start(bf16[64,64,128]{2,1,0:T(8,128)(2,1)S(1)} %all-to-all-done.same_ref), channel_id=1, source_target_pairs={{0,8},{8,0},{16,24},{24,16},{32,40},{40,32},{48,56},{56,48},{64,72... | collective-permute-start | bytes 3145736 | tf_op jit(solution)/shard_map/ppermute | solution.py:409
  53.8 17.2 %collective-permute-start.5 = (bf16[40,128,128]{2,1,0:T(8,128)(2,1)}, bf16[40,128,128]{2,1,0:T(8,128)(2,1)}, u32[]{:S(2)}, u32[]{:S(2)}) collective-permute-start(bf16[40,128,128]{2,1,0:T(8,128)(2,1)} %collective-permute-done.1), channel_id=1, source_target_pairs={{0,16},{1,17},{2,18},{3,19},{4,20},{5,21},{6,22},{7,23},{8,72},{9,... | collective-permute-start | bytes 3932168 | tf_op jit(solution)/shard_map/ppermute | solution.py:384
  53.8 23.3 %collective-permute-start.8 = (bf16[40,128,128]{2,1,0:T(8,128)(2,1)}, bf16[40,128,128]{2,1,0:T(8,128)(2,1)}, u32[]{:S(2)}, u32[]{:S(2)}) collective-permute-start(bf16[40,128,128]{2,1,0:T(8,128)(2,1)} %collective-permute-done.3), channel_id=1, source_target_pairs={{0,8},{8,0},{16,24},{24,16},{32,40},{40,32},{48,56},{56,48},{64,72... | collective-permute-start | bytes 3932168 | tf_op jit(solution)/shard_map/ppermute | solution.py:409
  54.2 22.9 %collective-permute-start.7 = (bf16[40,128,128]{2,1,0:T(8,128)(2,1)}, bf16[40,128,128]{2,1,0:T(8,128)(2,1)}, u32[]{:S(2)}, u32[]{:S(2)}) collective-permute-start(bf16[40,128,128]{2,1,0:T(8,128)(2,1)} %collective-permute-done.2), channel_id=1, source_target_pairs={{0,8},{8,0},{16,24},{24,16},{32,40},{40,32},{48,56},{56,48},{64,72... | collective-permute-start | bytes 3932168 | tf_op jit(solution)/shard_map/ppermute | solution.py:409
  54.3 22.8 %collective-permute-start.4 = (bf16[40,128,128]{2,1,0:T(8,128)(2,1)}, bf16[40,128,128]{2,1,0:T(8,128)(2,1)}, u32[]{:S(2)}, u32[]{:S(2)}) collective-permute-start(bf16[40,128,128]{2,1,0:T(8,128)(2,1)} %collective-permute-done.2), channel_id=1, source_target_pairs={{0,48},{1,49},{2,50},{3,51},{4,52},{5,53},{6,54},{7,55},{8,14},{9,... | collective-permute-start | bytes 3932168 | tf_op jit(solution)/shard_map/ppermute | solution.py:384
  62.0 15.1 %all-to-all-start.1 = ((f32[128,1,128]{2,1,0:T(1,128)}), f32[128,1,128]{2,1,0:T(1,128)S(1)}, u32[]{:S(2)}, u32[]{:S(2)}) async-start(f32[128,1,128]{2,1,0:T(1,128)} %broadcast_in_dim.8), calls=%async_computation.1 | async-start | bytes 131072 | tf_op jit(solution)/shard_map/all_to_all | solution.py:371
  77.1 18.7 %collective-permute-start.13 = (bf16[40,128,128]{2,1,0:T(8,128)(2,1)}, bf16[40,128,128]{2,1,0:T(8,128)(2,1)S(1)}, u32[]{:S(2)}, u32[]{:S(2)}) collective-permute-start(bf16[40,128,128]{2,1,0:T(8,128)(2,1)} %collective-permute-done.5), channel_id=1, source_target_pairs={{0,8},{8,0},{16,24},{24,16},{32,40},{40,32},{48,56},{56,48},{64,72... | collective-permute-start | bytes 3932168 | tf_op jit(solution)/shard_map/ppermute | solution.py:409
  78.3 18.2 %collective-permute-start.10 = (bf16[40,128,128]{2,1,0:T(8,128)(2,1)}, bf16[40,128,128]{2,1,0:T(8,128)(2,1)S(1)}, u32[]{:S(2)}, u32[]{:S(2)}) collective-permute-start(bf16[40,128,128]{2,1,0:T(8,128)(2,1)} %collective-permute-done.5), channel_id=1, source_target_pairs={{0,16},{1,17},{2,18},{3,19},{4,20},{5,21},{6,22},{7,23},{8,10},{9,... | collective-permute-start | bytes 3932168 | tf_op jit(solution)/shard_map/ppermute | solution.py:384
  78.8 17.0 %collective-permute-start.9 = (bf16[40,128,128]{2,1,0:T(8,128)(2,1)}, bf16[40,128,128]{2,1,0:T(8,128)(2,1)S(1)}, u32[]{:S(2)}, u32[]{:S(2)}) collective-permute-start(bf16[40,128,128]{2,1,0:T(8,128)(2,1)} %broadcast_select_fusion), channel_id=1, source_target_pairs={{0,48},{1,49},{2,50},{3,51},{4,52},{5,53},{6,54},{7,55},{8,14},{9,... | collective-permute-start | bytes 3932168 | tf_op jit(solution)/shard_map/ppermute | solution.py:384
  80.9 14.9 %collective-permute-start.11 = (bf16[40,128,128]{2,1,0:T(8,128)(2,1)}, bf16[40,128,128]{2,1,0:T(8,128)(2,1)S(1)}, u32[]{:S(2)}, u32[]{:S(2)}) collective-permute-start(bf16[40,128,128]{2,1,0:T(8,128)(2,1)} %collective-permute-done.4), channel_id=1, source_target_pairs={{0,8},{8,0},{16,24},{24,16},{32,40},{40,32},{48,56},{56,48},{64,72... | collective-permute-start | bytes 3932168 | tf_op jit(solution)/shard_map/ppermute | solution.py:409
  81.6 14.2 %collective-permute-start.12 = (bf16[40,128,128]{2,1,0:T(8,128)(2,1)}, bf16[40,128,128]{2,1,0:T(8,128)(2,1)S(1)}, u32[]{:S(2)}, u32[]{:S(2)}) collective-permute-start(bf16[40,128,128]{2,1,0:T(8,128)(2,1)} %collective-permute-done.1), channel_id=1, source_target_pairs={{0,8},{8,0},{16,24},{24,16},{32,40},{40,32},{48,56},{56,48},{64,72... | collective-permute-start | bytes 3932168 | tf_op jit(solution)/shard_map/ppermute | solution.py:409
  96.4 17.6 %collective-permute-start.18 = (bf16[40,128,128]{2,1,0:T(8,128)(2,1)S(1)}, bf16[40,128,128]{2,1,0:T(8,128)(2,1)S(1)}, u32[]{:S(2)}, u32[]{:S(2)}) collective-permute-start(bf16[40,128,128]{2,1,0:T(8,128)(2,1)S(1)} %collective-permute-done.10), channel_id=1, source_target_pairs={{0,8},{8,0},{16,24},{24,16},{32,40},{40,32},{48,56},{56,48},{64,72... | collective-permute-start | bytes 3932168 | tf_op jit(solution)/shard_map/ppermute | solution.py:409
  97.4 16.7 %collective-permute-start.17 = (bf16[40,128,128]{2,1,0:T(8,128)(2,1)S(1)}, bf16[40,128,128]{2,1,0:T(8,128)(2,1)S(1)}, u32[]{:S(2)}, u32[]{:S(2)}) collective-permute-start(bf16[40,128,128]{2,1,0:T(8,128)(2,1)S(1)} %collective-permute-done.9), channel_id=1, source_target_pairs={{0,8},{8,0},{16,24},{24,16},{32,40},{40,32},{48,56},{56,48},{64,72... | collective-permute-start | bytes 3932168 | tf_op jit(solution)/shard_map/ppermute | solution.py:409
  97.5 11.7 %collective-permute-start.15 = (bf16[20,128,128]{2,1,0:T(8,128)(2,1)S(1)}, bf16[20,128,128]{2,1,0:T(8,128)(2,1)S(1)}, u32[]{:S(2)}, u32[]{:S(2)}) collective-permute-start(bf16[20,128,128]{2,1,0:T(8,128)(2,1)S(1)} %slice.7), channel_id=1, source_target_pairs={{8,6},{9,7},{10,0},{11,1},{12,2},{13,3},{14,4},{15,5},{24,22},{25,... | collective-permute-start | bytes 1966088 | tf_op jit(solution)/shard_map/ppermute | solution.py:405
  101.5 12.5 %collective-permute-start.14 = (bf16[20,128,128]{2,1,0:T(8,128)(2,1)S(1)}, bf16[20,128,128]{2,1,0:T(8,128)(2,1)S(1)}, u32[]{:S(2)}, u32[]{:S(2)}) collective-permute-start(bf16[20,128,128]{2,1,0:T(8,128)(2,1)S(1)} %slice.6), channel_id=1, source_target_pairs={{8,10},{9,11},{10,12},{11,13},{12,14},{13,15},{14,8},{15,9},{24,26... | collective-permute-start | bytes 1966088 | tf_op jit(solution)/shard_map/ppermute | solution.py:405
  103.4 1.6 %collective-permute-start.16 = (bf16[4,128,128]{2,1,0:T(8,128)(2,1)S(1)}, bf16[4,128,128]{2,1,0:T(8,128)(2,1)S(1)}, u32[]{:S(2)}, u32[]{:S(2)}) collective-permute-start(bf16[4,128,128]{2,1,0:T(8,128)(2,1)S(1)} %grid_cols.1.col_own_ref), channel_id=1, source_target_pairs={{0,8},{8,0},{16,24},{24,16},{32,40},{40,32},{48,56},{56,48},{64,72... | collective-permute-start | bytes 393224 | tf_op jit(solution)/shard_map/ppermute | solution.py:409
  104.3 9.7 %copy-start.7 = (bf16[2560,128]{1,0:T(8,128)(2,1)S(1)}, bf16[2560,128]{1,0:T(8,128)(2,1)}, u32[]{:S(2)}) copy-start(bf16[2560,128]{1,0:T(8,128)(2,1)} %copy-done.6) | copy-start | bytes 1966084
  104.3 9.7 %copy-start.9 = (bf16[20,128,128]{2,1,0:T(8,128)(2,1)S(1)}, bf16[20,128,128]{2,1,0:T(8,128)(2,1)}, u32[]{:S(2)}) copy-start(bf16[20,128,128]{2,1,0:T(8,128)(2,1)} %copy-done.8) | copy-start | bytes 1966084
  (9 other events, 36.1 us)
where the time goes:
time: 130 us; the launch traced here: 129 us
  Pallas kernels  40.9 us (31%)
  starting transfers between devices  37.7 us (29%)
  waiting for transfers between devices  25.9 us (20%)
  between operations  15.5 us (12%)
  local copies, waits for them, and re-layouts  4.88 us (4%)
  other arithmetic  3.96 us (3%)
    all_to_all x2, waiting for transfers between devices, to_all(): return lax.all_to_all(copies, axis, 0, 0, axis_index_groups=groups)  12.2 us
    all_to_all x2, starting transfers between devices, to_all(): return lax.all_to_all(copies, axis, 0, 0, axis_index_groups=groups)  12.1 us
    ppermute x10, starting transfers between devices, to_core(): return lax.ppermute(value, 'row', [(k, k ^ 1) for k in range(16)])  10.3 us
    pallas_call x2, Pallas kernels, grid_blocks(): pl.pallas_call(functools.partial(grid_kernel, with_sum), in_specs=[SM, SM...  10.3 us
    pallas_call x1, Pallas kernels, body(): pl.pallas_call(values_kernel, in_specs=[SM, VM, VM, VM], out_specs=HBM, o...  10.3 us
    ppermute x7, starting transfers between devices, move(): lax.ppermute(value, ('row', 'col'), [(k, device_of(*where(*place_of(k))))...  9.46 us
    pallas_call x1, Pallas kernels, body(): pl.pallas_call(plan_kernel, in_specs=[SM, VM], out_specs=[SM] * 5, out_sh...  7.58 us
    pallas_call x1, Pallas kernels, sparse(): pl.pallas_call(product_kernel, in_specs=[SM] * 6 + [VM] * 2 + [ANY] * 18,...  7.06 us
  transfers between devices with their start and end apart: 21, of which 9 were waited for; matrix products, arithmetic and copies ran while one was open for 4% of the time, Pallas kernels for 25%

commit v1 on v0

--- a/solution.py
+++ b/solution.py
@@ -9,8 +9,8 @@
 
 BS = 128
 CAP = 20
-GROUP = 4
-TURN = 4
+GROUP = 2
+TURN = 8
 ORDER = 8192
 VOLUME = 0.015625
 SUM_LANE = 64

time: 130 us -> 130 us (level)
  transfers between devices with their start and end apart: 21 -> 21, of which waited for: 9 -> 9; matrix products, arithmetic and copies ran while one was open for 4% -> 4% of each run, Pallas kernels for 25% -> 26%
where the time goes in v1:
time: 130 us; the launch traced here: 129 us
  Pallas kernels  41.8 us (32%)
  starting transfers between devices  37.8 us (29%)
  waiting for transfers between devices  25.1 us (19%)
  between operations  15.5 us (12%)
  local copies, waits for them, and re-layouts  4.88 us (4%)
  other arithmetic  3.96 us (3%)
    all_to_all x2, waiting for transfers between devices, to_all(): return lax.all_to_all(copies, axis, 0, 0, axis_index_groups=groups)  12.2 us
    all_to_all x2, starting transfers between devices, to_all(): return lax.all_to_all(copies, axis, 0, 0, axis_index_groups=groups)  11.9 us
    ppermute x10, starting transfers between devices, to_core(): return lax.ppermute(value, 'row', [(k, k ^ 1) for k in range(16)])  10.4 us
    pallas_call x2, Pallas kernels, grid_blocks(): pl.pallas_call(functools.partial(grid_kernel, with_sum), in_specs=[SM, SM...  10.3 us
    pallas_call x1, Pallas kernels, body(): pl.pallas_call(values_kernel, in_specs=[SM, VM, VM, VM], out_specs=HBM, o...  10.3 us
    ppermute x7, starting transfers between devices, move(): lax.ppermute(value, ('row', 'col'), [(k, device_of(*where(*place_of(k))))...  9.5 us
    pallas_call x1, Pallas kernels, body(): pl.pallas_call(plan_kernel, in_specs=[SM, VM], out_specs=[SM] * 5, out_sh...  8.08 us
    pallas_call x1, Pallas kernels, sparse(): pl.pallas_call(product_kernel, in_specs=[SM] * 6 + [VM] * 2 + [ANY] * 18,...  7.13 us
  transfers between devices with their start and end apart: 21, of which 9 were waited for; matrix products, arithmetic and copies ran while one was open for 4% of the time, Pallas kernels for 26%

profile of v1, /device:TPU:1, one launch (start us, length us, event | category | flops | bytes accessed | tf_op | source)
XLA Modules:
  0.0 129.1 jit_solution(4688413098202947502)
XLA Ops:
  9.2 1.5 %pack.1 = (bf16[2560,128]{1,0:T(8,128)(2,1)S(1)}, f32[8,128]{1,0:T(8,128)S(1)}) custom-call(s32[4,8]{1,0:T(4,128)S(1)} %copy-done.10, s32[2]{0:T(128)S(1)} %pad_add_fusion.place_ref, bf16[512,1024]{1,0:T(8,128)(2,1)S(1)} %copy-done), custom_call_target="tpu_custom_call" | custom-call | flops 2000000000 | bytes 1048576 | tf_op jit(solution)/shard_map/pack/pallas_call | solution.py:434
  10.7 1.5 %collective-permute-start = (bf16[20,128,128]{2,1,0:T(8,128)(2,1)S(1)}, bf16[20,128,128]{2,1,0:T(8,128)(2,1)S(1)}, u32[]{:S(2)}, u32[]{:S(2)}) collective-permute-start(bf16[20,128,128]{2,1,0:T(8,128)(2,1)S(1)} %bitcast.18), channel_id=1, source_target_pairs={{0,8},{8,0},{16,24},{24,16},{32,40},{40,32},{48,56},{56,48},{64,72... | collective-permute-start | bytes 1966088 | tf_op jit(solution)/shard_map/ppermute | solution.py:409
  12.2 1.7 %collective-permute-done = bf16[20,128,128]{2,1,0:T(8,128)(2,1)S(1)} collective-permute-done((bf16[20,128,128]{2,1,0:T(8,128)(2,1)S(1)}, bf16[20,128,128]{2,1,0:T(8,128)(2,1)S(1)}, u32[]{:S(2)}, u32[]{:S(2)}) %collective-permute-start) | collective-permute-done | bytes 655392 | tf_op jit(solution)/shard_map/ppermute | solution.py:409
  15.2 1.8 %collective-permute-start.3 = (bf16[40,128,128]{2,1,0:T(8,128)(2,1)}, bf16[40,128,128]{2,1,0:T(8,128)(2,1)}, u32[]{:S(2)}, u32[]{:S(2)}) collective-permute-start(bf16[40,128,128]{2,1,0:T(8,128)(2,1)} %pad_maximum_fusion), channel_id=1, source_target_pairs={{0,16},{1,17},{2,18},{3,19},{4,20},{5,21},{6,22},{7,23},{8,10},{9,... | collective-permute-start | bytes 3932168 | tf_op jit(solution)/shard_map/ppermute | solution.py:384
  17.0 2.1 %collective-permute-start.2 = (bf16[40,128,128]{2,1,0:T(8,128)(2,1)}, bf16[40,128,128]{2,1,0:T(8,128)(2,1)}, u32[]{:S(2)}, u32[]{:S(2)}) collective-permute-start(bf16[40,128,128]{2,1,0:T(8,128)(2,1)} %pad_maximum_fusion), channel_id=1, source_target_pairs={{0,48},{1,49},{2,50},{3,51},{4,52},{5,53},{6,54},{7,55},{8,14},{9,... | collective-permute-start | bytes 3932168 | tf_op jit(solution)/shard_map/ppermute | solution.py:384
  19.1 2.8 %collective-permute-start.1 = (bf16[40,128,128]{2,1,0:T(8,128)(2,1)}, bf16[40,128,128]{2,1,0:T(8,128)(2,1)}, u32[]{:S(2)}, u32[]{:S(2)}) collective-permute-start(bf16[40,128,128]{2,1,0:T(8,128)(2,1)} %pad_maximum_fusion), channel_id=1, source_target_pairs={{0,64},{1,65},{2,66},{3,67},{4,68},{5,69},{6,70},{7,71},{8,73},{9,... | collective-permute-start | bytes 3932168 | tf_op jit(solution)/shard_map/ppermute | solution.py:384
  23.1 6.3 %all-to-all-start = ((bf16[64,64,128]{2,1,0:T(8,128)(2,1)}), bf16[64,64,128]{2,1,0:T(8,128)(2,1)S(1)}, u32[]{:S(2)}, u32[]{:S(2)}) async-start(bf16[64,64,128]{2,1,0:T(8,128)(2,1)} %broadcast_in_dim.6), calls=%async_computation | async-start | bytes 2097152 | tf_op jit(solution)/shard_map/all_to_all | solution.py:371
  29.5 10.3 %values.1.phi_ref = bf16[8,8,128,1024]{3,2,1,0:T(8,128)(2,1)} custom-call(s32[2]{0:T(128)S(1)} %pad_add_fusion.place_ref, s32[3,64,128]{2,1,0:T(8,128)S(1)} %copy-done.2, f32[64,128]{1,0:T(8,128)S(1)} %copy-done.4, s32[64,128]{1,0:T(8,128)S(1)} %copy-done.5), custom_call_target="tpu_custom_call" | custom-call | flops 10000000000 | bytes 1048576 | tf_op jit(solution)/shard_map/values/pallas_call | solution.py:449
  39.8 8.7 %all-to-all-done.same_ref = bf16[64,64,128]{2,1,0:T(8,128)(2,1)S(1)} async-done(((bf16[64,64,128]{2,1,0:T(8,128)(2,1)}), bf16[64,64,128]{2,1,0:T(8,128)(2,1)S(1)}, u32[]{:S(2)}, u32[]{:S(2)}) %all-to-all-start) | async-done | bytes 1048608 | tf_op jit(solution)/shard_map/all_to_all | solution.py:371
  48.4 5.4 %collective-permute-start.6 = (bf16[64,64,128]{2,1,0:T(8,128)(2,1)S(1)}, bf16[64,64,128]{2,1,0:T(8,128)(2,1)S(1)}, u32[]{:S(2)}, u32[]{:S(2)}) collective-permute-start(bf16[64,64,128]{2,1,0:T(8,128)(2,1)S(1)} %all-to-all-done.same_ref), channel_id=1, source_target_pairs={{0,8},{8,0},{16,24},{24,16},{32,40},{40,32},{48,56},{56,48},{64,72... | collective-permute-start | bytes 3145736 | tf_op jit(solution)/shard_map/ppermute | solution.py:409
  56.2 5.3 %grid_rows.1 = (bf16[4,128,128]{2,1,0:T(8,128)(2,1)S(1)}, f32[1,128]{1,0:T(1,128)S(1)}) custom-call(s32[2]{0:T(128)S(1)} %pad_add_fusion.place_ref, s32[64]{0:T(128)S(1)} %copy-done.1, f32[1]{0:T(128)S(6)} %copy.14.shift_ref, bf16[64,64,128]{2,1,0:T(8,128)(2,1)S(1)} %all-to-all-done.same_ref, bf16[64,64,128]{2,1,0:T(8,128)(2,1)S(1)} %collective-permute-done.6.other_ref, ...), custom_call_target="tpu_custom_call" | custom-call | flops 5000000000 | bytes 1048576 | tf_op jit(solution)/shard_map/grid_rows/pallas_call | solution.py:475
  62.1 5.6 %all-to-all-start.1 = ((f32[128,1,128]{2,1,0:T(1,128)}), f32[128,1,128]{2,1,0:T(1,128)S(1)}, u32[]{:S(2)}, u32[]{:S(2)}) async-start(f32[128,1,128]{2,1,0:T(1,128)} %broadcast_in_dim.8), calls=%async_computation.1 | async-start | bytes 131072 | tf_op jit(solution)/shard_map/all_to_all | solution.py:371
  67.7 3.4 %collective-permute-done.5 = bf16[40,128,128]{2,1,0:T(8,128)(2,1)} collective-permute-done((bf16[40,128,128]{2,1,0:T(8,128)(2,1)}, bf16[40,128,128]{2,1,0:T(8,128)(2,1)}, u32[]{:S(2)}, u32[]{:S(2)}) %collective-permute-start.5) | collective-permute-done | bytes 1310752 | tf_op jit(solution)/shard_map/ppermute | solution.py:384
  71.0 2.6 %broadcast_select_fusion = bf16[40,128,128]{2,1,0:T(8,128)(2,1)} fusion(bf16[40,128,128]{2,1,0:T(8,128)(2,1)} %collective-permute-done.1, bf16[40,128,128]{2,1,0:T(8,128)(2,1)} %collective-permute-done.5, pred[]{:T(512)S(6)} %eq.5), kind=kLoop, calls=%fused_computation.3 | loop fusion | flops 655360 | bytes 3932161 | tf_op jit(solution)/shard_map/jit(_where)/select_n | solution.py:489
  73.6 3.5 %all-to-all-done.1 = f32[128,1,128]{2,1,0:T(1,128)S(1)} async-done(((f32[128,1,128]{2,1,0:T(1,128)}), f32[128,1,128]{2,1,0:T(1,128)S(1)}, u32[]{:S(2)}, u32[]{:S(2)}) %all-to-all-start.1) | async-done | bytes 65568 | tf_op jit(solution)/shard_map/all_to_all | solution.py:371
  78.9 2.1 %collective-permute-start.9 = (bf16[40,128,128]{2,1,0:T(8,128)(2,1)}, bf16[40,128,128]{2,1,0:T(8,128)(2,1)S(1)}, u32[]{:S(2)}, u32[]{:S(2)}) collective-permute-start(bf16[40,128,128]{2,1,0:T(8,128)(2,1)} %broadcast_select_fusion), channel_id=1, source_target_pairs={{0,48},{1,49},{2,50},{3,51},{4,52},{5,53},{6,54},{7,55},{8,14},{9,... | collective-permute-start | bytes 3932168 | tf_op jit(solution)/shard_map/ppermute | solution.py:384
  81.6 5.0 %grid_cols.1.col_own_ref = bf16[4,128,128]{2,1,0:T(8,128)(2,1)S(1)} custom-call(s32[2]{0:T(128)S(1)} %pad_add_fusion.place_ref, s32[64]{0:T(128)S(1)} %copy-done.1, f32[1]{0:T(128)S(6)} %copy.14.shift_ref, bf16[64,64,128]{2,1,0:T(8,128)(2,1)S(1)} %all-to-all-done.same_ref, bf16[64,64,128]{2,1,0:T(8,128)(2,1)S(1)} %collective-permute-done.6.other_ref, ...), custom_call_target="tpu_custom_call" | custom-call | flops 5000000000 | bytes 1048576 | tf_op jit(solution)/shard_map/grid_cols/pallas_call | solution.py:475
  86.7 8.1 %plan.1 = (s32[1]{0:T(128)}, s32[1064]{0:T(1024)S(1)}, s32[2128]{0:T(1024)S(1)}, s32[2128]{0:T(1024)S(1)}, s32[1]{0:T(128)}) custom-call(s32[2]{0:T(128)S(1)} %pad_add_fusion.place_ref, f32[128,128]{1,0:T(8,128)S(1)} %bitcast.21), custom_call_target="tpu_custom_call" | custom-call | flops 8999999488 | bytes 1048576 | tf_op jit(solution)/shard_map/plan/pallas_call | solution.py:499
  97.5 4.0 %collective-permute-start.15 = (bf16[20,128,128]{2,1,0:T(8,128)(2,1)S(1)}, bf16[20,128,128]{2,1,0:T(8,128)(2,1)S(1)}, u32[]{:S(2)}, u32[]{:S(2)}) collective-permute-start(bf16[20,128,128]{2,1,0:T(8,128)(2,1)S(1)} %slice.7), channel_id=1, source_target_pairs={{8,6},{9,7},{10,0},{11,1},{12,2},{13,3},{14,4},{15,5},{24,22},{25,... | collective-permute-start | bytes 1966088 | tf_op jit(solution)/shard_map/ppermute | solution.py:405
  101.5 1.9 %collective-permute-start.14 = (bf16[20,128,128]{2,1,0:T(8,128)(2,1)S(1)}, bf16[20,128,128]{2,1,0:T(8,128)(2,1)S(1)}, u32[]{:S(2)}, u32[]{:S(2)}) collective-permute-start(bf16[20,128,128]{2,1,0:T(8,128)(2,1)S(1)} %slice.6), channel_id=1, source_target_pairs={{8,10},{9,11},{10,12},{11,13},{12,14},{13,15},{14,8},{15,9},{24,26... | collective-permute-start | bytes 1966088 | tf_op jit(solution)/shard_map/ppermute | solution.py:405
  105.1 4.5 %prepare.1 = (bf16[512,1024]{1,0:T(8,128)(2,1)}, f32[32,128,128]{2,1,0:T(8,128)S(1)}) custom-call(s32[2]{0:T(128)S(1)} %pad_add_fusion.place_ref, s32[4,8]{1,0:T(4,128)S(1)} %copy-done.10, f32[1]{0:T(128)S(6)} %copy.14.shift_ref, f32[128,128]{1,0:T(8,128)S(1)} %bitcast.22, bf16[512,1024]{1,0:T(8,128)(2,1)S(1)} %copy-done, ...), custom_call_target="tpu_custom_call" | custom-call | flops 4000000000 | bytes 1048576 | tf_op jit(solution)/shard_map/prepare/pallas_call | solution.py:525
  109.6 4.5 %collective-permute-done.14 = bf16[20,128,128]{2,1,0:T(8,128)(2,1)S(1)} collective-permute-done((bf16[20,128,128]{2,1,0:T(8,128)(2,1)S(1)}, bf16[20,128,128]{2,1,0:T(8,128)(2,1)S(1)}, u32[]{:S(2)}, u32[]{:S(2)}) %collective-permute-start.14) | collective-permute-done | bytes 655392 | tf_op jit(solution)/shard_map/ppermute | solution.py:405
  114.1 7.2 %conditional.1 = (bf16[512,1024]{1,0:T(8,128)(2,1)S(1)}) conditional(s32[]{:T(128)} %bitcast.6, (s32[2]{0:T(128)S(1)}, s32[4,8]{1,0:T(4,128)S(1)}, s32[1]{0:T(128)}, s32[1064]{0:T(1024)S(1)}, s32[2128]{0:T(1024)S(1)}, /*index=5*/s32[2128]{0:T(1024)S(1)}, f32[128,128]{1,0:T(8,128)S(1)}, f32[32,128,128]{2,1,0:T(8,128)S(1)}, ...), branch_computations={%region_0.1_spmd, %region_1.2_spmd} | conditional | flops 12000000000 | bytes 112198104 | solution.py:567
  114.1 7.1 %product.1 = bf16[512,1024]{1,0:T(8,128)(2,1)S(1)} custom-call(s32[2]{0:T(128)S(1)} %get-tuple-element.56.place_ref, s32[4,8]{1,0:T(4,128)S(1)} %get-tuple-element.60.pattern_ref, s32[1]{0:T(128)} %get-tuple-element.61.turns_ref, s32[1064]{0:T(1024)S(1)} %get-tuple-element.62.out_ref, s32[2128]{0:T(1024)S(1)} %get-tuple-element.63.left_ref, ...), custom_call_target="tpu_custom_call" | custom-call | flops 12000000000 | bytes 1048576 | tf_op jit(solution)/shard_map/cond/branch_0_fun/product/pallas_call | solution.py:542
  (58 shorter events, 13.9 us)
Async XLA Ops:
  10.7 3.2 %collective-permute-start = (bf16[20,128,128]{2,1,0:T(8,128)(2,1)S(1)}, bf16[20,128,128]{2,1,0:T(8,128)(2,1)S(1)}, u32[]{:S(2)}, u32[]{:S(2)}) collective-permute-start(bf16[20,128,128]{2,1,0:T(8,128)(2,1)S(1)} %bitcast.18), channel_id=1, source_target_pairs={{0,8},{8,0},{16,24},{24,16},{32,40},{40,32},{48,56},{56,48},{64,72... | collective-permute-start | bytes 1966088 | tf_op jit(solution)/shard_map/ppermute | solution.py:409
  15.2 33.2 %collective-permute-start.3 = (bf16[40,128,128]{2,1,0:T(8,128)(2,1)}, bf16[40,128,128]{2,1,0:T(8,128)(2,1)}, u32[]{:S(2)}, u32[]{:S(2)}) collective-permute-start(bf16[40,128,128]{2,1,0:T(8,128)(2,1)} %pad_maximum_fusion), channel_id=1, source_target_pairs={{0,16},{1,17},{2,18},{3,19},{4,20},{5,21},{6,22},{7,23},{8,10},{9,... | collective-permute-start | bytes 3932168 | tf_op jit(solution)/shard_map/ppermute | solution.py:384
  17.0 31.4 %collective-permute-start.2 = (bf16[40,128,128]{2,1,0:T(8,128)(2,1)}, bf16[40,128,128]{2,1,0:T(8,128)(2,1)}, u32[]{:S(2)}, u32[]{:S(2)}) collective-permute-start(bf16[40,128,128]{2,1,0:T(8,128)(2,1)} %pad_maximum_fusion), channel_id=1, source_target_pairs={{0,48},{1,49},{2,50},{3,51},{4,52},{5,53},{6,54},{7,55},{8,14},{9,... | collective-permute-start | bytes 3932168 | tf_op jit(solution)/shard_map/ppermute | solution.py:384
  19.1 29.3 %collective-permute-start.1 = (bf16[40,128,128]{2,1,0:T(8,128)(2,1)}, bf16[40,128,128]{2,1,0:T(8,128)(2,1)}, u32[]{:S(2)}, u32[]{:S(2)}) collective-permute-start(bf16[40,128,128]{2,1,0:T(8,128)(2,1)} %pad_maximum_fusion), channel_id=1, source_target_pairs={{0,64},{1,65},{2,66},{3,67},{4,68},{5,69},{6,70},{7,71},{8,73},{9,... | collective-permute-start | bytes 3932168 | tf_op jit(solution)/shard_map/ppermute | solution.py:384
  23.1 25.3 %all-to-all-start = ((bf16[64,64,128]{2,1,0:T(8,128)(2,1)}), bf16[64,64,128]{2,1,0:T(8,128)(2,1)S(1)}, u32[]{:S(2)}, u32[]{:S(2)}) async-start(bf16[64,64,128]{2,1,0:T(8,128)(2,1)} %broadcast_in_dim.6), calls=%async_computation | async-start | bytes 2097152 | tf_op jit(solution)/shard_map/all_to_all | solution.py:371
  29.5 26.7 %copy-start.1 = (s32[64]{0:T(128)S(1)}, s32[64]{0:T(128)}, u32[]{:S(2)}) copy-start(s32[64]{0:T(128)} %home_ref.3) | copy-start | bytes 772
  48.4 7.7 %collective-permute-start.6 = (bf16[64,64,128]{2,1,0:T(8,128)(2,1)S(1)}, bf16[64,64,128]{2,1,0:T(8,128)(2,1)S(1)}, u32[]{:S(2)}, u32[]{:S(2)}) collective-permute-start(bf16[64,64,128]{2,1,0:T(8,128)(2,1)S(1)} %all-to-all-done.same_ref), channel_id=1, source_target_pairs={{0,8},{8,0},{16,24},{24,16},{32,40},{40,32},{48,56},{56,48},{64,72... | collective-permute-start | bytes 3145736 | tf_op jit(solution)/shard_map/ppermute | solution.py:409
  53.9 17.2 %collective-permute-start.5 = (bf16[40,128,128]{2,1,0:T(8,128)(2,1)}, bf16[40,128,128]{2,1,0:T(8,128)(2,1)}, u32[]{:S(2)}, u32[]{:S(2)}) collective-permute-start(bf16[40,128,128]{2,1,0:T(8,128)(2,1)} %collective-permute-done.1), channel_id=1, source_target_pairs={{0,16},{1,17},{2,18},{3,19},{4,20},{5,21},{6,22},{7,23},{8,72},{9,... | collective-permute-start | bytes 3932168 | tf_op jit(solution)/shard_map/ppermute | solution.py:384
  53.9 23.3 %collective-permute-start.8 = (bf16[40,128,128]{2,1,0:T(8,128)(2,1)}, bf16[40,128,128]{2,1,0:T(8,128)(2,1)}, u32[]{:S(2)}, u32[]{:S(2)}) collective-permute-start(bf16[40,128,128]{2,1,0:T(8,128)(2,1)} %collective-permute-done.3), channel_id=1, source_target_pairs={{0,8},{8,0},{16,24},{24,16},{32,40},{40,32},{48,56},{56,48},{64,72... | collective-permute-start | bytes 3932168 | tf_op jit(solution)/shard_map/ppermute | solution.py:409
  54.2 23.0 %collective-permute-start.7 = (bf16[40,128,128]{2,1,0:T(8,128)(2,1)}, bf16[40,128,128]{2,1,0:T(8,128)(2,1)}, u32[]{:S(2)}, u32[]{:S(2)}) collective-permute-start(bf16[40,128,128]{2,1,0:T(8,128)(2,1)} %collective-permute-done.2), channel_id=1, source_target_pairs={{0,8},{8,0},{16,24},{24,16},{32,40},{40,32},{48,56},{56,48},{64,72... | collective-permute-start | bytes 3932168 | tf_op jit(solution)/shard_map/ppermute | solution.py:409
  54.4 22.8 %collective-permute-start.4 = (bf16[40,128,128]{2,1,0:T(8,128)(2,1)}, bf16[40,128,128]{2,1,0:T(8,128)(2,1)}, u32[]{:S(2)}, u32[]{:S(2)}) collective-permute-start(bf16[40,128,128]{2,1,0:T(8,128)(2,1)} %collective-permute-done.2), channel_id=1, source_target_pairs={{0,48},{1,49},{2,50},{3,51},{4,52},{5,53},{6,54},{7,55},{8,14},{9,... | collective-permute-start | bytes 3932168 | tf_op jit(solution)/shard_map/ppermute | solution.py:384
  62.1 15.1 %all-to-all-start.1 = ((f32[128,1,128]{2,1,0:T(1,128)}), f32[128,1,128]{2,1,0:T(1,128)S(1)}, u32[]{:S(2)}, u32[]{:S(2)}) async-start(f32[128,1,128]{2,1,0:T(1,128)} %broadcast_in_dim.8), calls=%async_computation.1 | async-start | bytes 131072 | tf_op jit(solution)/shard_map/all_to_all | solution.py:371
  77.2 18.7 %collective-permute-start.13 = (bf16[40,128,128]{2,1,0:T(8,128)(2,1)}, bf16[40,128,128]{2,1,0:T(8,128)(2,1)S(1)}, u32[]{:S(2)}, u32[]{:S(2)}) collective-permute-start(bf16[40,128,128]{2,1,0:T(8,128)(2,1)} %collective-permute-done.5), channel_id=1, source_target_pairs={{0,8},{8,0},{16,24},{24,16},{32,40},{40,32},{48,56},{56,48},{64,72... | collective-permute-start | bytes 3932168 | tf_op jit(solution)/shard_map/ppermute | solution.py:409
  78.3 18.2 %collective-permute-start.10 = (bf16[40,128,128]{2,1,0:T(8,128)(2,1)}, bf16[40,128,128]{2,1,0:T(8,128)(2,1)S(1)}, u32[]{:S(2)}, u32[]{:S(2)}) collective-permute-start(bf16[40,128,128]{2,1,0:T(8,128)(2,1)} %collective-permute-done.5), channel_id=1, source_target_pairs={{0,16},{1,17},{2,18},{3,19},{4,20},{5,21},{6,22},{7,23},{8,10},{9,... | collective-permute-start | bytes 3932168 | tf_op jit(solution)/shard_map/ppermute | solution.py:384
  78.9 17.0 %collective-permute-start.9 = (bf16[40,128,128]{2,1,0:T(8,128)(2,1)}, bf16[40,128,128]{2,1,0:T(8,128)(2,1)S(1)}, u32[]{:S(2)}, u32[]{:S(2)}) collective-permute-start(bf16[40,128,128]{2,1,0:T(8,128)(2,1)} %broadcast_select_fusion), channel_id=1, source_target_pairs={{0,48},{1,49},{2,50},{3,51},{4,52},{5,53},{6,54},{7,55},{8,14},{9,... | collective-permute-start | bytes 3932168 | tf_op jit(solution)/shard_map/ppermute | solution.py:384
  81.0 14.9 %collective-permute-start.11 = (bf16[40,128,128]{2,1,0:T(8,128)(2,1)}, bf16[40,128,128]{2,1,0:T(8,128)(2,1)S(1)}, u32[]{:S(2)}, u32[]{:S(2)}) collective-permute-start(bf16[40,128,128]{2,1,0:T(8,128)(2,1)} %collective-permute-done.4), channel_id=1, source_target_pairs={{0,8},{8,0},{16,24},{24,16},{32,40},{40,32},{48,56},{56,48},{64,72... | collective-permute-start | bytes 3932168 | tf_op jit(solution)/shard_map/ppermute | solution.py:409
  81.6 14.2 %collective-permute-start.12 = (bf16[40,128,128]{2,1,0:T(8,128)(2,1)}, bf16[40,128,128]{2,1,0:T(8,128)(2,1)S(1)}, u32[]{:S(2)}, u32[]{:S(2)}) collective-permute-start(bf16[40,128,128]{2,1,0:T(8,128)(2,1)} %collective-permute-done.1), channel_id=1, source_target_pairs={{0,8},{8,0},{16,24},{24,16},{32,40},{40,32},{48,56},{56,48},{64,72... | collective-permute-start | bytes 3932168 | tf_op jit(solution)/shard_map/ppermute | solution.py:409
  96.5 17.6 %collective-permute-start.18 = (bf16[40,128,128]{2,1,0:T(8,128)(2,1)S(1)}, bf16[40,128,128]{2,1,0:T(8,128)(2,1)S(1)}, u32[]{:S(2)}, u32[]{:S(2)}) collective-permute-start(bf16[40,128,128]{2,1,0:T(8,128)(2,1)S(1)} %collective-permute-done.10), channel_id=1, source_target_pairs={{0,8},{8,0},{16,24},{24,16},{32,40},{40,32},{48,56},{56,48},{64,72... | collective-permute-start | bytes 3932168 | tf_op jit(solution)/shard_map/ppermute | solution.py:409
  97.4 16.7 %collective-permute-start.17 = (bf16[40,128,128]{2,1,0:T(8,128)(2,1)S(1)}, bf16[40,128,128]{2,1,0:T(8,128)(2,1)S(1)}, u32[]{:S(2)}, u32[]{:S(2)}) collective-permute-start(bf16[40,128,128]{2,1,0:T(8,128)(2,1)S(1)} %collective-permute-done.9), channel_id=1, source_target_pairs={{0,8},{8,0},{16,24},{24,16},{32,40},{40,32},{48,56},{56,48},{64,72... | collective-permute-start | bytes 3932168 | tf_op jit(solution)/shard_map/ppermute | solution.py:409
  97.5 12.0 %collective-permute-start.15 = (bf16[20,128,128]{2,1,0:T(8,128)(2,1)S(1)}, bf16[20,128,128]{2,1,0:T(8,128)(2,1)S(1)}, u32[]{:S(2)}, u32[]{:S(2)}) collective-permute-start(bf16[20,128,128]{2,1,0:T(8,128)(2,1)S(1)} %slice.7), channel_id=1, source_target_pairs={{8,6},{9,7},{10,0},{11,1},{12,2},{13,3},{14,4},{15,5},{24,22},{25,... | collective-permute-start | bytes 1966088 | tf_op jit(solution)/shard_map/ppermute | solution.py:405
  101.5 12.5 %collective-permute-start.14 = (bf16[20,128,128]{2,1,0:T(8,128)(2,1)S(1)}, bf16[20,128,128]{2,1,0:T(8,128)(2,1)S(1)}, u32[]{:S(2)}, u32[]{:S(2)}) collective-permute-start(bf16[20,128,128]{2,1,0:T(8,128)(2,1)S(1)} %slice.6), channel_id=1, source_target_pairs={{8,10},{9,11},{10,12},{11,13},{12,14},{13,15},{14,8},{15,9},{24,26... | collective-permute-start | bytes 1966088 | tf_op jit(solution)/shard_map/ppermute | solution.py:405
  103.5 1.6 %collective-permute-start.16 = (bf16[4,128,128]{2,1,0:T(8,128)(2,1)S(1)}, bf16[4,128,128]{2,1,0:T(8,128)(2,1)S(1)}, u32[]{:S(2)}, u32[]{:S(2)}) collective-permute-start(bf16[4,128,128]{2,1,0:T(8,128)(2,1)S(1)} %grid_cols.1.col_own_ref), channel_id=1, source_target_pairs={{0,8},{8,0},{16,24},{24,16},{32,40},{40,32},{48,56},{56,48},{64,72... | collective-permute-start | bytes 393224 | tf_op jit(solution)/shard_map/ppermute | solution.py:409
  104.4 9.7 %copy-start.7 = (bf16[2560,128]{1,0:T(8,128)(2,1)S(1)}, bf16[2560,128]{1,0:T(8,128)(2,1)}, u32[]{:S(2)}) copy-start(bf16[2560,128]{1,0:T(8,128)(2,1)} %copy-done.6) | copy-start | bytes 1966084
  104.4 9.7 %copy-start.9 = (bf16[20,128,128]{2,1,0:T(8,128)(2,1)S(1)}, bf16[20,128,128]{2,1,0:T(8,128)(2,1)}, u32[]{:S(2)}) copy-start(bf16[20,128,128]{2,1,0:T(8,128)(2,1)} %copy-done.8) | copy-start | bytes 1966084
  (9 other events, 35.8 us)
